TPU v7x, 32 devices: a whole 2x2x4 slice. The times are simulated.
32 devices in a mesh: groups: 2 (over y), blk: 4 (over z), probe: 2 (over x), sub: 2 (over core).
Axes of the slice: x: 2, y: 2, z: 4, core: 2. Of those that a mesh axis runs over, the one named last changes fastest.
Arguments:
- coords: float32 [3, 16384], P(None, ('groups', 'blk')), parts along dimension 1, may hold values from -4 to 4
- noise_var: float32 [16384], P(('groups', 'blk')), parts along dimension 0, may hold values from 0.5 to 2
- probe_signs: int32 [64, 16384], P('probe', ('groups', 'blk')), parts along dimension 1, may hold values from -1 to 1, as said below
- tile_rows: int32 [8, 2, 96], P(('groups', 'blk'), 'sub'), parts along dimension 0, may hold values from 0 to 15
- tile_cols: int32 [8, 2, 96], P(('groups', 'blk'), 'sub'), parts along dimension 0, may hold values from 0 to 31, as said below
- tile_count: int32 [8, 2], P(('groups', 'blk'), 'sub'), parts along dimension 0, may hold values from 24 to 96
Outputs:
- alphas: float32 [3, 128], P(None, ('groups', 'probe')), parts along dimension 1
- betas: float32 [3, 128], P(None, ('groups', 'probe')), parts along dimension 1
- last_basis: float32 [64, 16384], P('probe', ('groups', 'blk')), parts along dimension 1
- coord_grad: float32 [3, 16384], P(None, ('groups', 'blk')), parts along dimension 1
There are 2 independent parts, one for each index of `groups`. A program takes and returns all parts, laid end to end along the dimension named above; each array names one. Nothing has to cross between parts.
Inputs may be any that keep to these rules, and one draw needn't show every extreme that they name: `probe_signs`: every entry is -1 or 1. tile_cols minus tile_rows lies between 0 and 16 in every slot.
All inputs are finite; a program needn't handle non-finite values.
Results may differ from a plain program's by a relative error of at most 0.00025.
Values sent between devices are 32-bit elements; how exact they have to be, the bound alone decides.
No kernel may reach another device: no remote copies, remote signals or barrier semaphores. Data moves between devices by JAX's collectives and lax.ppermute only.
A program may use at most 64 MiB of HBM per device.

v0:
```python
import functools
import math

import jax
import jax.numpy as jnp
from jax import lax
from jax.experimental import pallas as pl
from jax.experimental.pallas import tpu as pltpu
from jax.sharding import PartitionSpec as P

ITERS = 3
SIGNAL_VAR = 0.1
LENGTH_SQ = 2.0
TAPER_SQ = 16.0
WARP_GAIN = 0.4
EPSILON = 1e-06

BLK = 128
LANES = 128
FEATS = 32
GROUP = 16
TAIL = 8
LIST_ROWS = 8
LIMIT_MIB = 16
KEPT = 256
WORK_FIRST = 300000000
WORK_NEXT = 100000000
WORK_BYTES = 4000000

DECAY = TAPER_SQ / (2.0 * LENGTH_SQ)
Z_TOP = math.sqrt(SIGNAL_VAR * math.exp(-DECAY))
Z_RATE = DECAY / Z_TOP
Z_OF_D = -Z_TOP / TAPER_SQ
Z_STEP = 4.0 * LENGTH_SQ / TAPER_SQ * Z_TOP

F32 = jnp.float32
BF16 = jnp.bfloat16


def split_two(x):
    high = x.astype(BF16)
    low = (x - high.astype(F32)).astype(BF16)
    return high, low


def split_three(x):
    one = x.astype(BF16).astype(F32)
    rest = x - one
    two = rest.astype(BF16).astype(F32)
    three = (rest - two).astype(BF16).astype(F32)
    return one, two, three


def warp(x):
    return x + WARP_GAIN * jnp.tanh(x)


def mxu(a, b):
    return lax.dot_general(a, b, (((1,), (0,)), ((), ())), preferred_element_type=F32)


def put_stats(ref, base, w_of, q_of, qq, qw, blocks):
    alpha_s = qw / jnp.maximum(qq, 1e-30)
    acc = jnp.zeros((qq.shape[0], LANES), F32)
    for b in range(blocks):
        r = w_of(b) - alpha_s * q_of(b)
        acc = acc + r * r
    res = jnp.sum(acc, axis=1, keepdims=True)
    lane = lax.broadcasted_iota(jnp.int32, (qq.shape[0], LANES), 1)
    out = jnp.where(lane == 0, qw, jnp.where(lane == 1, qq, jnp.where(lane == 2, res, 0.0)))
    ref[:, base : base + LANES] = out


def mxu_turned(a, b):
    return lax.dot_general(a, b, (((1,), (1,)), ((), ())), preferred_element_type=F32)


def fold(out, probes):
    if out.shape[0] > probes:
        return out[:probes] + out[probes:]
    return out


def fold_turned(out, probes):
    total = out[:probes, :BLK] + out[:probes, BLK:]
    if out.shape[0] > probes:
        total = total + out[probes:, :BLK]
    return total


def stack_vec(q, exact):
    if exact:
        high = q.astype(BF16)
        return jnp.concatenate([high, high], axis=1)
    high, low = split_two(q)
    return jnp.concatenate(
        [jnp.concatenate([high, high], axis=1), jnp.concatenate([low, jnp.zeros_like(low)], axis=1)], axis=0
    )


def stack_tile(tile):
    return jnp.concatenate(split_two(tile), axis=0)


def ranges(first, last, body):
    long = (last - first) // GROUP
    middle = first + long * GROUP

    def big(g, carry):
        body(first + g * GROUP, GROUP)
        return carry

    def small(g, carry):
        body(middle + g * TAIL, TAIL)
        return carry

    lax.fori_loop(0, long, big, 0)
    lax.fori_loop(0, (last - middle) // TAIL, small, 0)


def kept_and_made(total, room, body, kept, made):
    first = jnp.minimum(total, room)
    ranges(0, first, functools.partial(body, kept))
    many = (total - first) // TAIL

    def rest(g, carry):
        body(made, first + g * TAIL, TAIL)
        return carry

    lax.fori_loop(0, many, rest, 0)


def inner_edges(acc, vecs, plan, kept, made):
    acc[...] = jnp.zeros_like(acc)
    size = acc.shape[1]

    def group(tile_of, start, many):
        outs = []
        for u in range(many):
            slot = start + u
            a = plan[0, slot]
            c = plan[1, slot]
            times = plan[2, slot].astype(F32)
            tile = tile_of(slot, a, c)
            outs.append((c, fold(mxu(vecs[a], tile), size) * times))
            outs.append((a, fold_turned(mxu_turned(vecs[c][:, :BLK], tile), size) * times))
        for c, out in outs:
            acc[c] = acc[c] + out

    kept_and_made(plan[3, 0], KEPT, group, kept, made)


def outer_edges(acc, vecs, plan, base, kept, made):
    size = acc.shape[1]

    def group(tile_of, start, many):
        outs = []
        for u in range(many):
            at = start + u
            a = plan[0, at]
            c = plan[1, at]
            times = plan[2, at].astype(F32)
            outs.append((c, fold(mxu(vecs[a], tile_of(base + at, a, c)), size) * times))
        for c, out in outs:
            acc[c] = acc[c] + out

    kept_and_made(plan[3, 0], jnp.maximum(KEPT - base, 0), group, kept, made)


def tile_value(z):
    z = jnp.maximum(z, 0.0)
    return jnp.exp(z * Z_RATE) * (z * z)


def slope_value(z):
    z = jnp.maximum(z, 0.0)
    return (jnp.exp(z * Z_RATE) * z) * (z + Z_STEP)


def fill(into, base, plan, make):
    def body(start, many):
        for u in range(many):
            at = start + u
            into[base + at] = make(base + at, plan[0, at], plan[1, at])

    ranges(0, jnp.minimum(plan[3, 0], jnp.maximum(KEPT - base, 0)), body)


def maker(left, right):
    return lambda slot, a, c: stack_tile(tile_value(mxu(left[a], right[c])))


def keeper(tiles):
    return lambda slot, a, c: tiles[slot]


def whole(n):
    return jnp.floor((n + (TAIL - 1)) * (1.0 / TAIL)) * TAIL


def keys(lists, blocks, cross):
    out = []
    whole_lists = lists.astype(jnp.int32)
    for at in (0, 3):
        a = whole_lists[at : at + 1]
        c = whole_lists[at + 1 : at + 2]
        live = lax.broadcasted_iota(jnp.int32, a.shape, 1) < whole_lists[at + 2 : at + 3]
        if cross:
            out.append(jnp.where(live & (c >= blocks), a * blocks + c - blocks, -1))
        else:
            out.append(jnp.where(live & (c < blocks), a * blocks + c, -1))
    return jnp.concatenate(out, axis=1)


def compact(key, blocks, slots, first):
    size = blocks * blocks
    hot = jnp.where(lax.broadcasted_iota(jnp.int32, (size, key.shape[1]), 0) == key, 1.0, 0.0).astype(BF16)
    counts = mxu(hot, jnp.ones((key.shape[1], LANES), BF16))
    flags = jnp.minimum(counts, 1.0)
    shape = (size, size)
    ahead = lax.broadcasted_iota(jnp.int32, shape, 0) > lax.broadcasted_iota(jnp.int32, shape, 1)
    place = mxu(jnp.where(ahead, 1.0, 0.0).astype(BF16), flags.astype(BF16)) + first
    index = lax.broadcasted_iota(jnp.int32, (16, size), 1).astype(F32)
    row = jnp.floor((index + 0.5) * (1.0 / blocks))
    line = lax.broadcasted_iota(jnp.int32, (16, size), 0)
    names = jnp.where(line == 0, row, jnp.where(line == 1, index - row * blocks, 1.0)).astype(BF16)
    found = []
    times = []
    for part in range(slots // LANES):
        lane = (lax.broadcasted_iota(jnp.int32, (size, LANES), 1) + part * LANES).astype(F32)
        here = (place == lane) & (flags > 0.5)
        found.append(mxu(names, jnp.where(here, 1.0, 0.0).astype(BF16)))
        times.append(mxu(names, jnp.where(here, counts, 0.0).astype(BF16))[2:3])
    found = jnp.concatenate(found, axis=1)
    end = place[size - 1 :] + flags[size - 1 :]
    return found[0:1], found[1:2], found[2:3], jnp.concatenate(times, axis=1), end


def put_plan(ref, rows):
    ref[...] = jnp.zeros(ref.shape, ref.dtype)
    for at, row in enumerate(rows):
        ref[at : at + 1, :] = row.astype(ref.dtype)


def spread(row, width):
    return jnp.concatenate([row] * (width // LANES), axis=1)


def side_features(blocks, coords, kinds, left, right):
    x = warp(coords)
    scale = -2.0 * Z_OF_D
    square = x * x
    norm = Z_OF_D * (square[:blocks] + square[blocks : 2 * blocks] + square[2 * blocks :])
    x1, x2, x3 = split_three(x)
    n1, n2, n3 = split_three(norm)
    m1, m2, m3 = split_three(norm + Z_TOP)
    one = jnp.ones_like(norm)
    pad = jnp.zeros(((FEATS - 24) * blocks, BLK), F32)
    kinds[...] = jnp.concatenate([x1, x1, x2, x2, x1, x3, n1, n2, n3, one, one, one, pad], axis=0)
    for g in range(0, blocks, 4):
        stack = [kinds[pl.ds(b, FEATS, stride=blocks), :] for b in range(g, g + 4)]
        turned = jnp.concatenate(stack, axis=0).T.astype(BF16)
        for b in range(4):
            left[g + b] = turned[:, b * FEATS : (b + 1) * FEATS]
    if right is not None:
        y1, y2, y3 = split_three(x * scale)
        kinds[...] = jnp.concatenate([y1, y2, y1, y2, y3, y1, one, one, one, m1, m2, m3, pad], axis=0)
        for b in range(blocks):
            right[b] = kinds[pl.ds(b, FEATS, stride=blocks), :].astype(BF16)


def rows_of(packed, blocks):
    lists = packed.shape[0] - LIST_ROWS
    coords = lists - 3 * blocks
    return coords // blocks, coords, lists


def pack_kernel(
    blocks, place, tile_rows, tile_cols, tile_count, signs, coords, noise,
    lists, mine, noise_here, got_signs, got_coords, got_rows, got_cols, sems,
):
    probes, coord_row, list_row = rows_of(mine, blocks)
    first = pl.multiple_of(place[1] * probes, probes)
    moves = [
        pltpu.make_async_copy(coords, got_coords, sems.at[0]),
        pltpu.make_async_copy(signs.at[pl.ds(first, probes), :], got_signs, sems.at[1]),
        pltpu.make_async_copy(tile_rows, got_rows, sems.at[2]),
        pltpu.make_async_copy(tile_cols, got_cols, sems.at[3]),
        pltpu.make_async_copy(noise, noise_here, sems.at[4]),
    ]
    for move in moves:
        move.start()
    lists[...] = jnp.zeros(lists.shape, F32)
    lists[2:3, :] = jnp.full((1, LANES), tile_count[0], jnp.int32).astype(F32)
    for move in moves[2:4]:
        move.wait()
    lists[0:1, : tile_rows.shape[1]] = got_rows[...].astype(F32)
    lists[1:2, : tile_cols.shape[1]] = got_cols[...].astype(F32)
    mine[list_row:] = lists[...]
    moves[0].wait()
    for c in range(3):
        for b in range(blocks):
            at = coord_row + c * blocks + b
            mine[at : at + 1] = got_coords[c : c + 1, b * BLK : (b + 1) * BLK]
    moves[1].wait()
    for b in range(blocks):
        mine[b * probes : (b + 1) * probes] = got_signs[:, b * BLK : (b + 1) * BLK].astype(F32)
    moves[4].wait()


def join_kernel(sibling, old, mine):
    del old
    at = mine.shape[0] - LIST_ROWS + 3
    mine[at : at + 3] = sibling[0:3]


def first_inner_kernel(
    blocks, mine,
    plan, tiles, z_ref, cross, left, right, acc, vecs, held_plan, kinds, sem,
):
    probes, coord_row, list_row = rows_of(mine, blocks)
    lists = mine[list_row:]
    row, col, _, times, end = compact(keys(lists, blocks, False), blocks, held_plan.shape[1], 0.0)
    put_plan(held_plan, (row, col, times, spread(whole(end), held_plan.shape[1])))
    move = pltpu.make_async_copy(held_plan, plan, sem)
    move.start()
    row, col, _, times, end = compact(keys(lists, blocks, True), blocks, cross.shape[1], 0.0)
    put_plan(cross, (col, row, times, spread(end, cross.shape[1])))
    for b in range(blocks):
        vecs[b] = stack_vec(mine[b * probes : (b + 1) * probes], True)
    side_features(blocks, mine[coord_row:list_row], kinds, left, right)
    move.wait()
    fill(tiles, 0, plan, maker(left, right))
    inner_edges(acc, vecs, plan, keeper(tiles), maker(left, right))
    z_ref[...] = acc[:blocks]


def finish_apply(blocks, acc, z_of, w_ref, q_of, prev_of, beta, noise):
    probes = acc.shape[1]
    qq = jnp.zeros((probes, LANES), F32)
    qw = jnp.zeros((probes, LANES), F32)
    for b in range(blocks):
        q = q_of(b)
        part = slice(b * BLK, (b + 1) * BLK)
        w = acc[b] + z_of(b) + noise[b : b + 1] * q
        if prev_of is not None:
            w = w - beta * prev_of(b)
        w_ref[:, part] = w
        qq = qq + q * q
        qw = qw + q * w
    put_stats(
        w_ref,
        blocks * BLK,
        lambda b: w_ref[:, b * BLK : (b + 1) * BLK],
        q_of,
        jnp.sum(qq, axis=1, keepdims=True),
        jnp.sum(qw, axis=1, keepdims=True),
        blocks,
    )


def first_outer_kernel(
    blocks, inner_plan, old_tiles, mine, above, below, noise, z_ref, right, cross,
    plan, tiles, w_ref, left, acc, vecs, held_plan, kinds, sem,
):
    probes, coord_row, list_row = rows_of(mine, blocks)
    del old_tiles
    slots = held_plan.shape[1]
    row, col, one, times, end = compact(keys(below[list_row:], blocks, True), blocks, slots, cross[3:4, :LANES])
    put_plan(
        held_plan,
        (cross[0:1] + row + blocks * one, cross[1:2] + col, cross[2:3] + times, spread(whole(end), slots)),
    )
    move = pltpu.make_async_copy(held_plan, plan, sem)
    move.start()
    for part, ref in enumerate((above, below)):
        side_features(blocks, ref[coord_row:list_row], kinds, left.at[part * blocks : (part + 1) * blocks], None)
        for b in range(blocks):
            vecs[part * blocks + b] = stack_vec(ref[b * probes : (b + 1) * probes], True)
    acc[...] = jnp.zeros_like(acc)
    move.wait()
    base = inner_plan[3, 0]
    fill(tiles, base, plan, maker(left, right))
    outer_edges(acc, vecs, plan, base, keeper(tiles), maker(left, right))
    finish_apply(
        blocks, acc, lambda b: z_ref[b], w_ref, lambda b: mine[b * probes : (b + 1) * probes], None, None, noise
    )


def slab_alpha(w_ref, blocks):
    sums = w_ref[:, blocks * BLK : (blocks + 1) * BLK]
    return sums[:, 0:1] / jnp.maximum(sums[:, 1:2], 1e-30)


def inner_kernel(blocks, plan, w_ref, q_own, tiles, left, right, z_ref, acc, vecs):
    alpha = slab_alpha(w_ref, blocks)
    probes = w_ref.shape[0]
    for b in range(blocks):
        vecs[b] = stack_vec(w_ref[:, b * BLK : (b + 1) * BLK] - alpha * block_of(q_own, probes, b), False)
    inner_edges(acc, vecs, plan, keeper(tiles), maker(left, right))
    z_ref[...] = acc[:blocks]


def alpha_beta(stats, points):
    qw = [s[:, 0:1] for s in stats]
    qq = [s[:, 1:2] for s in stats]
    res = [s[:, 2:3] for s in stats]
    alpha = functools.reduce(jnp.add, qw) / points
    total = jnp.zeros_like(alpha)
    for w, q, r in zip(qw, qq, res):
        gap = alpha - w / jnp.maximum(q, 1e-30)
        total = total + (r + gap * gap * q)
    return alpha, jnp.sqrt(total / points + EPSILON)


def global_alpha_beta(slabs, points, place, stats_ref):
    order = [stats_ref[lax.rem(slab - place[0] + slabs, slabs)] for slab in range(slabs)]
    return alpha_beta(order, points)


def add_ab(ref, base, old_ab, step, alpha, beta):
    shape = (alpha.shape[0], LANES)
    lane = lax.broadcasted_iota(jnp.int32, shape, 1)
    out = jnp.zeros(shape, F32) if old_ab is None else old_ab[...]
    out = jnp.where(lane == step, alpha, out)
    ref[:, base : base + LANES] = jnp.where(lane == ITERS + step, beta, out)


def block_of(ref, rows, b):
    if len(ref.shape) == 3:
        return ref[b]
    return ref[b * rows : (b + 1) * rows]


def outer_kernel(
    blocks, slabs, points, step, place, inner_plan, plan, mine, above, below, stats_ref,
    q_own, q_above, q_below, z_raw, z_old, noise, tiles, left, right, *rest,
):
    probes = mine.shape[0]
    old_ab = None
    if step > 0:
        old_ab = rest[0]
        rest = rest[1:]
    w_ref, own_ref, above_ref, below_ref, ab_ref, *z_ref, acc, vecs, held_z = rest
    alpha, beta = global_alpha_beta(slabs, points, place, stats_ref)
    scale = 1.0 / beta
    apart = alpha - slab_alpha(mine, blocks)
    add_ab(ab_ref, 0, old_ab, step, alpha, beta)
    halves = ((mine, q_own, own_ref), (above, q_above, above_ref), (below, q_below, below_ref))
    for part, (w, old, new) in enumerate(halves):
        for b in range(blocks):
            q = (w[:, b * BLK : (b + 1) * BLK] - alpha * block_of(old, probes, b)) * scale
            new[b] = q
            if part > 0:
                vecs[(part - 1) * blocks + b] = stack_vec(q, False)
            else:
                z = (z_raw[b] - apart * z_old[b]) * scale
                held_z[b] = z
                for ref in z_ref:
                    ref[b] = z
    acc[...] = jnp.zeros_like(acc)
    outer_edges(acc, vecs, plan, inner_plan[3, 0], keeper(tiles), maker(left, right))
    finish_apply(
        blocks, acc, lambda b: held_z[b], w_ref, lambda b: own_ref[b], lambda b: block_of(q_own, probes, b), beta, noise
    )


def slope_kernel(inner_plan, plan, left_own, left_halo, right, after, slopes):
    del after

    def make(left):
        return lambda slot, a, c: slope_value(mxu(left[a], right[c]))

    fill(slopes, 0, inner_plan, make(left_own))
    fill(slopes, inner_plan[3, 0], plan, make(left_halo))


def points_kernel(blocks, pts, pts_above, pts_below, after, pnts, halo_pnts, slack, kinds):
    del after
    _, coord_row, list_row = rows_of(pts, blocks)
    for part, ref in enumerate((pts, pts_above, pts_below)):
        raw = ref[coord_row:list_row]
        bent = jnp.tanh(raw)
        x = raw + WARP_GAIN * bent
        x1, x2, x3 = split_three(x)
        one = jnp.ones((blocks, BLK), F32)
        kinds[...] = jnp.concatenate([x1, x2, x3, one, jnp.zeros((6 * blocks, BLK), F32)], axis=0)
        if part == 0:
            slack[...] = jnp.concatenate([x, 1.0 + WARP_GAIN * (1.0 - bent * bent)], axis=0)
        for b in range(blocks):
            y = kinds[pl.ds(b, 16, stride=blocks), :].astype(BF16)
            y = jnp.concatenate([y, y], axis=1)
            if part == 0:
                pnts[b] = y
            else:
                halo_pnts[(part - 1) * blocks + b] = y


def last_kernel(
    blocks, slabs, points, all_probes, place, inner_plan, plan, mine, above, below, stats_ref,
    q_own, q_above, q_below, pts, pts_above, pts_below, old_ab, slopes, left_own, left_out, right, pnts, halo_pnts, slack,
    out_ref, acc, form_left, halo_left, form_right, pulls,
):
    probes, _, _ = rows_of(pts, blocks)
    alpha, beta = global_alpha_beta(slabs, points, place, stats_ref)
    scale = 1.0 / beta
    out_ref[probes:, blocks * BLK :] = jnp.zeros((3, LANES), F32)
    add_ab(out_ref.at[:probes], blocks * BLK, old_ab, ITERS - 1, alpha, beta)
    for part, (w, old, ref) in enumerate(((mine, q_own, pts), (above, q_above, pts_above), (below, q_below, pts_below))):
        for b in range(blocks):
            part_cols = slice(b * BLK, (b + 1) * BLK)
            u = (w[:, part_cols] - alpha * block_of(old, probes, b)) * scale
            v = ref[b * probes : (b + 1) * probes]
            high = u.astype(BF16).astype(F32)
            low = u - high
            turned = jnp.concatenate([high, low, v, v], axis=0).T.astype(BF16)
            if part == 0:
                out_ref[:probes, part_cols] = u
                form_left[b] = turned
                form_right[b] = jnp.concatenate([v, v, high, low], axis=0).astype(BF16)
            else:
                halo_left[(part - 1) * blocks + b] = turned

    def pull(side):
        return lambda slot, a, c: stack_tile(mxu(side[a], form_right[c]) * slopes[slot])

    def pull_made(side, left):
        return lambda slot, a, c: stack_tile(mxu(side[a], form_right[c]) * slope_value(mxu(left[a], right[c])))

    base = inner_plan[3, 0]
    fill(pulls, 0, inner_plan, pull(form_left))
    fill(pulls, base, plan, pull(halo_left))
    inner_edges(acc, pnts, inner_plan, keeper(pulls), pull_made(form_left, left_own))
    outer_edges(acc, halo_pnts, plan, base, keeper(pulls), pull_made(halo_left, left_out))
    for b in range(blocks):
        part_cols = slice(b * BLK, (b + 1) * BLK)
        x = slack[pl.ds(b, 3, stride=blocks), :]
        chain = slack[pl.ds(3 * blocks + b, 3, stride=blocks), :]
        sums = acc[b]
        moved = sums[0:3] + sums[3:6] + sums[6:9] - x * sums[9:10]
        out_ref[probes:, part_cols] = moved * chain * (1.0 / (LENGTH_SQ * all_probes))


def pair_kernel(own, other, grad_ref):
    probes = own.shape[0] - 3
    width = grad_ref.shape[1]
    grad_ref[...] = own[probes:, :width] + other[probes:, :width]


def close_kernel(place, own, other, basis_ref, alpha_ref, beta_ref):
    probes = own.shape[0] - 3
    width = basis_ref.shape[1]
    lower = place[1] == 0
    mine = own[:probes]
    theirs = other[:probes]
    first = jnp.where(lower, mine, theirs)
    second = jnp.where(lower, theirs, mine)
    basis_ref[:probes] = first[:, :width]
    basis_ref[probes:] = second[:, :width]
    ab = jnp.concatenate([first[:, width:], second[:, width:]], axis=0)
    turned = jnp.concatenate([ab, jnp.zeros((LANES - 2 * probes, LANES), F32)], axis=0).T
    alpha_ref[...] = turned[:ITERS, : 2 * probes]
    beta_ref[...] = turned[ITERS : 2 * ITERS, : 2 * probes]


def vmem(count):
    return [pl.BlockSpec(memory_space=pltpu.VMEM)] * count


def smem(count):
    return [pl.BlockSpec(memory_space=pltpu.SMEM)] * count


def held(array):
    return pltpu.with_memory_space_constraint(array, pltpu.VMEM)


def stays(array):
    return pltpu.with_memory_space_constraint(array, pltpu.HBM)


def in_hbm(count):
    return [pl.BlockSpec(memory_space=pltpu.HBM)] * count


def call(name, kernel, outs, ins, scratch, work, aliases=None, limit=LIMIT_MIB):
    out_shapes, out_scalars = outs
    arrays, scalars = ins
    flops, moved = work
    return pl.pallas_call(
        kernel,
        out_shape=tuple(out_shapes),
        in_specs=smem(scalars) + vmem(len(arrays) - scalars),
        out_specs=tuple(smem(out_scalars) + vmem(len(out_shapes) - out_scalars)),
        scratch_shapes=[pltpu.VMEM(*entry) if isinstance(entry, tuple) else entry for entry in scratch],
        compiler_params=pltpu.CompilerParams(vmem_limit_bytes=limit * 1024 * 1024),
        cost_estimate=pl.CostEstimate(flops=flops, bytes_accessed=moved, transcendentals=0),
        input_output_aliases=aliases or {},
        name=name,
    )(*arrays)


def shifted(value, axes, count, steps):
    return lax.ppermute(value, axes, [(source, (source + steps) % count) for source in range(count)])


def body(coords, noise_var, probe_signs, tile_rows, tile_cols, tile_count):
    slabs = lax.axis_size("blk")
    subs = lax.axis_size("sub")
    outer = lax.axis_size("probe")
    probes = probe_signs.shape[0] // subs
    width = coords.shape[1]
    blocks = width // BLK
    cap = tile_rows.shape[-1]
    points = float(width * slabs)
    all_probes = probe_signs.shape[0] * outer
    sub = lax.axis_index("sub")
    blk = lax.axis_index("blk")
    place = jnp.stack([blk, sub]).astype(jnp.int32)
    sds = jax.ShapeDtypeStruct

    left_shape = sds((blocks, BLK, FEATS), BF16)
    right_shape = sds((blocks, FEATS, BLK), BF16)
    packed = sds((blocks * (probes + 3) + LIST_ROWS, BLK), F32)
    kinds = ((blocks * FEATS, BLK), F32)
    lists, own, noise = pl.pallas_call(
        functools.partial(pack_kernel, blocks),
        out_shape=(sds((LIST_ROWS, LANES), F32), packed, sds((blocks, BLK), F32)),
        in_specs=smem(1) + in_hbm(2) + smem(1) + in_hbm(3),
        out_specs=tuple(vmem(3)),
        scratch_shapes=[
            pltpu.VMEM((probes, width), jnp.int32),
            pltpu.VMEM((3, width), F32),
            pltpu.VMEM((1, cap), jnp.int32),
            pltpu.VMEM((1, cap), jnp.int32),
            pltpu.SemaphoreType.DMA((5,)),
        ],
        compiler_params=pltpu.CompilerParams(vmem_limit_bytes=LIMIT_MIB * 1024 * 1024),
        name="pack",
    )(
        place, stays(tile_rows.reshape(1, cap)), stays(tile_cols.reshape(1, cap)), tile_count.reshape(1),
        stays(probe_signs), stays(coords), stays(noise_var.reshape(blocks, BLK)),
    )
    sibling = shifted(lists, "sub", subs, 1)
    (mine,) = call("join", join_kernel, ((packed,), 0), ((sibling, own), 0), [], (1000, 1000), {1: 0})
    above = shifted(mine, "blk", slabs, -1)
    below = shifted(mine, "blk", slabs, 1)

    ints = jnp.int32
    inner_slots = (blocks * (blocks + 1) // 2 + TAIL + LANES - 1) // LANES * LANES
    outer_slots = (blocks * (blocks + 1) + TAIL + LANES - 1) // LANES * LANES
    plan_shape = sds((LIST_ROWS, inner_slots), ints)
    outer_plan_shape = sds((LIST_ROWS, outer_slots), ints)
    slots = KEPT
    ext = width + LANES
    blocks_f32 = sds((blocks, probes, BLK), F32)
    tile_shape = pltpu.VMEM((slots, 2 * BLK, BLK), BF16)
    acc_shape = ((blocks, probes, BLK), F32)

    inner_plan, tiles, z, cross, left_own, right = call(
        "first_inner",
        functools.partial(first_inner_kernel, blocks),
        ((plan_shape, tile_shape, blocks_f32, sds((LIST_ROWS, outer_slots), F32), left_shape, right_shape), 1),
        ((mine,), 0),
        [
            acc_shape, ((blocks, probes, 2 * BLK), BF16), ((LIST_ROWS, inner_slots), ints), kinds,
            pltpu.SemaphoreType.DMA,
        ],
        (WORK_FIRST, WORK_BYTES),
    )
    outer_plan, tiles, w, left_halo = call(
        "first_outer",
        functools.partial(first_outer_kernel, blocks),
        ((outer_plan_shape, tile_shape, sds((probes, ext), F32), sds((2 * blocks, BLK, FEATS), BF16)), 1),
        ((inner_plan, held(tiles), mine, above, below, noise, z, right, cross), 1),
        [
            acc_shape, ((2 * blocks, probes, 2 * BLK), BF16), ((LIST_ROWS, outer_slots), ints), kinds,
            pltpu.SemaphoreType.DMA,
        ],
        (WORK_FIRST, WORK_BYTES),
        {1: 1},
    )

    def exchange(w):
        stats = w[:, width:]
        if slabs == 4:
            far = shifted(stats, "blk", slabs, 2)
        up = shifted(w, "blk", slabs, -1)
        down = shifted(w, "blk", slabs, 1)
        if slabs == 4:
            rows = jnp.stack([stats, up[:, width:], far, down[:, width:]])
        else:
            rows = lax.all_gather(stats, "blk", axis=0)
            rows = jnp.roll(rows, -blk, axis=0)
        return up, down, rows

    q = (mine, above, below)
    ab = []
    z_old = z
    for step in range(ITERS - 1):
        up, down, stats = exchange(w)
        (z_raw,) = call(
            "inner",
            functools.partial(inner_kernel, blocks),
            ((blocks_f32,), 0),
            ((inner_plan, w, q[0], held(tiles), left_own, right), 1),
            [acc_shape, ((blocks, 2 * probes, 2 * BLK), BF16)],
            (WORK_NEXT, WORK_BYTES),
        )
        w, q0, q1, q2, next_ab, *z = call(
            "outer",
            functools.partial(outer_kernel, blocks, slabs, points, step),
            (
                (
                    sds((probes, ext), F32), blocks_f32, blocks_f32, blocks_f32, sds((probes, LANES), F32),
                    *([blocks_f32] if step < ITERS - 2 else []),
                ),
                0,
            ),
            ((place, inner_plan, outer_plan, w, up, down, stats, *q, z_raw, z_old, noise, held(tiles), left_halo, right, *ab), 3),
            [acc_shape, ((2 * blocks, 2 * probes, 2 * BLK), BF16), ((blocks, probes, BLK), F32)],
            (WORK_NEXT, WORK_BYTES),
        )
        q = (q0, q1, q2)
        ab = [next_ab]
        z_old = z[0] if z else None

    up, down, stats = exchange(w)
    (slopes,) = call(
        "slopes",
        slope_kernel,
        ((pltpu.VMEM((slots, BLK, BLK), F32),), 0),
        ((inner_plan, outer_plan, left_own, left_halo, right, w), 2),
        [],
        (WORK_FIRST, WORK_BYTES),
    )
    pnts, halo_pnts, slack = call(
        "points",
        functools.partial(points_kernel, blocks),
        (
            (
                sds((blocks, 16, 2 * BLK), BF16), sds((2 * blocks, 16, 2 * BLK), BF16), sds((6 * blocks, BLK), F32),
            ),
            0,
        ),
        ((mine, above, below, w), 0),
        [((blocks * 16, BLK), F32)],
        (WORK_NEXT, WORK_BYTES),
    )
    (result,) = call(
        "last",
        functools.partial(last_kernel, blocks, slabs, points, all_probes),
        ((sds((probes + 3, ext), F32),), 0),
        (
            (
                place, inner_plan, outer_plan, w, up, down, stats, *q, mine, above, below, *ab, held(slopes), left_own, left_halo,
                right, pnts, halo_pnts, slack,
            ),
            3,
        ),
        [
            ((blocks, 16, BLK), F32),
            ((blocks, BLK, 4 * probes), BF16),
            ((2 * blocks, BLK, 4 * probes), BF16),
            ((blocks, 4 * probes, BLK), BF16),
            ((slots, 2 * BLK, BLK), BF16),
        ],
        (WORK_FIRST, WORK_BYTES),
        limit=LIMIT_MIB * 3 // 2,
    )

    other = shifted(result, "sub", subs, 1)
    (grad,) = call("pair", pair_kernel, ((sds((3, width), F32),), 0), ((result, other), 0), [], (1000, 1000))
    if outer == 2:
        coord_grad = grad + shifted(grad, "probe", outer, 1)
    else:
        coord_grad = lax.psum(grad, "probe")
    last_basis, alphas, betas = call(
        "close",
        close_kernel,
        (
            (
                sds((subs * probes, width), F32), sds((ITERS, subs * probes), F32), sds((ITERS, subs * probes), F32),
            ),
            0,
        ),
        ((place, result, other), 1),
        [],
        (1000000, 1000000),
    )
    return alphas, betas, last_basis, coord_grad


def solution(mesh):
    return jax.shard_map(
        body,
        mesh=mesh,
        in_specs=(
            P(None, ("groups", "blk")),
            P(("groups", "blk")),
            P("probe", ("groups", "blk")),
            P(("groups", "blk"), "sub", None),
            P(("groups", "blk"), "sub", None),
            P(("groups", "blk"), "sub"),
        ),
        out_specs=(
            P(None, ("groups", "probe")),
            P(None, ("groups", "probe")),
            P("probe", ("groups", "blk")),
            P(None, ("groups", "blk")),
        ),
        check_vma=False,
    )
```

profile of v0, /device:TPU:0, one launch (start us, length us, event | category | flops | bytes accessed | tf_op | source)
XLA Modules:
  0.0 72.5 jit_solution(7513656170898731216)
XLA Ops:
  1.4 1.5 %pack.1 = (f32[8,128]{1,0:T(8,128)S(1)}, f32[312,128]{1,0:T(8,128)S(1)}, f32[16,128]{1,0:T(8,128)S(1)}) custom-call(s32[2]{0:T(128)S(1)} %pad_add_fusion.place, s32[1,96]{1,0:T(1,128)} %bitcast.32, s32[1,96]{1,0:T(1,128)} %bitcast.33, s32[1]{0:T(128)} %bitcast.27.tile_count, s32[32,2048]{1,0:T(8,128)} %signs.1, f32[3,2048]{1,0:T(4,128)} %coords.1, ...), custom_call_target="tpu_custom_call" | custom-call | tf_op jit(solution)/shard_map/pack/pallas_call | solution.py:626
  2.9 0.5 collective-permute-start
  3.4 0.8 %collective-permute-done.sibling = f32[8,128]{1,0:T(8,128)S(1)} collective-permute-done((f32[8,128]{1,0:T(8,128)S(1)}, f32[8,128]{1,0:T(8,128)S(1)}, u32[]{:S(2)}, u32[]{:S(2)}) %collective-permute-start) | collective-permute-done | bytes 4128 | tf_op jit(solution)/shard_map/ppermute | solution.py:604
  4.2 2.9 %collective-permute-start.2 = (f32[312,128]{1,0:T(8,128)S(1)}, f32[312,128]{1,0:T(8,128)S(1)}, u32[]{:S(2)}, u32[]{:S(2)}) collective-permute-start(f32[312,128]{1,0:T(8,128)S(1)} %join.1.mine.q_own.pts), channel_id=1, source_target_pairs={{0,4},{4,8},{8,12},{12,0},{1,5},{5,9},{9,13},{13,1},{2,6},{6,10},{... | collective-permute-start | bytes 479240 | tf_op jit(solution)/shard_map/ppermute | solution.py:604
  7.1 2.0 %collective-permute-start.1 = (f32[312,128]{1,0:T(8,128)S(1)}, f32[312,128]{1,0:T(8,128)S(1)}, u32[]{:S(2)}, u32[]{:S(2)}) collective-permute-start(f32[312,128]{1,0:T(8,128)S(1)} %join.1.mine.q_own.pts), channel_id=1, source_target_pairs={{0,12},{4,0},{8,4},{12,8},{1,13},{5,1},{9,5},{13,9},{2,14},{6,2},{... | collective-permute-start | bytes 479240 | tf_op jit(solution)/shard_map/ppermute | solution.py:604
  9.2 4.8 %first_inner.1 = (s32[8,256]{1,0:T(8,128)S(1)}, bf16[256,256,128]{2,1,0:T(8,128)(2,1)S(1)}, f32[16,16,128]{2,1,0:T(8,128)S(1)}, f32[8,384]{1,0:T(8,128)S(1)}, bf...) custom-call(f32[312,128]{1,0:T(8,128)S(1)} %join.1.mine.q_own.pts), custom_call_target="tpu_custom_call" | custom-call | flops 300000000 | bytes 4000000 | tf_op jit(solution)/shard_map/first_inner/pallas_call | solution.py:590
  14.0 0.1 collective-permute-done.2.below.q_below.pts_below
  14.1 2.4 %collective-permute-done.1.above.q_above.pts_above = f32[312,128]{1,0:T(8,128)S(1)} collective-permute-done((f32[312,128]{1,0:T(8,128)S(1)}, f32[312,128]{1,0:T(8,128)S(1)}, u32[]{:S(2)}, u32[]{:S(2)}) %collective-permute-start.1) | collective-permute-done | bytes 159776 | tf_op jit(solution)/shard_map/ppermute | solution.py:604
  16.5 7.7 %first_outer.1 = (s32[8,384]{1,0:T(8,128)S(1)}, bf16[256,256,128]{2,1,0:T(8,128)(2,1)S(1)}, f32[16,2176]{1,0:T(8,128)S(1)}, bf16[32,128,32]{2,1,0:T(8,128)(2,1)S(1)}) custom-call(s32[8,256]{1,0:T(8,128)S(1)} %get-tuple-element.36.inner_plan.plan, bf16[256,256,128]{2,1,0:T(8,128)(2,1)S(1)} %get-tuple-element.37.old_tiles, ...), custom_call_target="tpu_custom_call", output_to_operand_aliasing={{1}: (1, {})} | custom-call | flops 300000000 | bytes 4000000 | tf_op jit(solution)/shard_map/first_outer/pallas_call | solution.py:590
  24.1 1.4 %collective-permute-start.4 = (f32[16,2176]{1,0:T(8,128)S(1)}, f32[16,2176]{1,0:T(8,128)S(1)}, u32[]{:S(2)}, u32[]{:S(2)}) collective-permute-start(f32[16,2176]{1,0:T(8,128)S(1)} %get-tuple-element.43.w_ref.mine), channel_id=1, source_target_pairs={{0,4},{4,8},{8,12},{12,0},{1,5},{5,9},{9,13},{13,1},{2,6},{6,10},{... | collective-permute-start | bytes 417800 | tf_op jit(solution)/shard_map/ppermute | solution.py:604
  25.5 2.5 %collective-permute-start.3 = (f32[16,2176]{1,0:T(8,128)S(1)}, f32[16,2176]{1,0:T(8,128)S(1)}, u32[]{:S(2)}, u32[]{:S(2)}) collective-permute-start(f32[16,2176]{1,0:T(8,128)S(1)} %get-tuple-element.43.w_ref.mine), channel_id=1, source_target_pairs={{0,12},{4,0},{8,4},{12,8},{1,13},{5,1},{9,5},{13,9},{2,14},{6,2},{... | collective-permute-start | bytes 417800 | tf_op jit(solution)/shard_map/ppermute | solution.py:604
  28.0 2.6 %inner.2.z_raw = f32[16,16,128]{2,1,0:T(8,128)S(1)} custom-call(s32[8,256]{1,0:T(8,128)S(1)} %get-tuple-element.36.inner_plan.plan, f32[16,2176]{1,0:T(8,128)S(1)} %get-tuple-element.43.w_ref.mine, f32[312,128]{1,0:T(8,128)S(1)} %join.1.mine.q_own.pts, bf16[256,256,128]{2,1,0:T(8,128)(2,1)S(1)} %get-tuple-element.44.tiles, ...), custom_call_target="tpu_custom_call" | custom-call | flops 100000000 | bytes 4000000 | tf_op jit(solution)/shard_map/inner/pallas_call | solution.py:590
  30.6 2.0 %collective-permute-done.4.below = f32[16,2176]{1,0:T(8,128)S(1)} collective-permute-done((f32[16,2176]{1,0:T(8,128)S(1)}, f32[16,2176]{1,0:T(8,128)S(1)}, u32[]{:S(2)}, u32[]{:S(2)}) %collective-permute-start.4) | collective-permute-done | bytes 139296 | tf_op jit(solution)/shard_map/ppermute | solution.py:604
  32.6 1.4 %collective-permute-done.3.above = f32[16,2176]{1,0:T(8,128)S(1)} collective-permute-done((f32[16,2176]{1,0:T(8,128)S(1)}, f32[16,2176]{1,0:T(8,128)S(1)}, u32[]{:S(2)}, u32[]{:S(2)}) %collective-permute-start.3) | collective-permute-done | bytes 139296 | tf_op jit(solution)/shard_map/ppermute | solution.py:604
  34.0 3.5 %outer.2 = (f32[16,2176]{1,0:T(8,128)S(1)}, f32[16,16,128]{2,1,0:T(8,128)S(1)}, f32[16,16,128]{2,1,0:T(8,128)S(1)}, f32[16,16,128]{2,1,0:T(8,128)S(1)}, f32[16,1...) custom-call(s32[2]{0:T(128)S(1)} %pad_add_fusion.place, s32[8,256]{1,0:T(8,128)S(1)} %get-tuple-element.36.inner_plan.plan, ...), custom_call_target="tpu_custom_call" | custom-call | flops 100000000 | bytes 4000000 | tf_op jit(solution)/shard_map/outer/pallas_call | solution.py:590
  37.5 0.8 %collective-permute-start.7 = (f32[16,2176]{1,0:T(8,128)S(1)}, f32[16,2176]{1,0:T(8,128)S(1)}, u32[]{:S(2)}, u32[]{:S(2)}) collective-permute-start(f32[16,2176]{1,0:T(8,128)S(1)} %get-tuple-element.47.w_ref.mine), channel_id=1, source_target_pairs={{0,4},{4,8},{8,12},{12,0},{1,5},{5,9},{9,13},{13,1},{2,6},{6,10},{... | collective-permute-start | bytes 417800 | tf_op jit(solution)/shard_map/ppermute | solution.py:604
  38.3 3.0 %collective-permute-start.6 = (f32[16,2176]{1,0:T(8,128)S(1)}, f32[16,2176]{1,0:T(8,128)S(1)}, u32[]{:S(2)}, u32[]{:S(2)}) collective-permute-start(f32[16,2176]{1,0:T(8,128)S(1)} %get-tuple-element.47.w_ref.mine), channel_id=1, source_target_pairs={{0,12},{4,0},{8,4},{12,8},{1,13},{5,1},{9,5},{13,9},{2,14},{6,2},{... | collective-permute-start | bytes 417800 | tf_op jit(solution)/shard_map/ppermute | solution.py:604
  41.3 2.6 %inner.3.z_raw = f32[16,16,128]{2,1,0:T(8,128)S(1)} custom-call(s32[8,256]{1,0:T(8,128)S(1)} %get-tuple-element.36.inner_plan.plan, f32[16,2176]{1,0:T(8,128)S(1)} %get-tuple-element.47.w_ref.mine, f32[16,16,128]{2,1,0:T(8,128)S(1)} %get-tuple-element.48.q_own, bf16[256,256,128]{2,1,0:T(8,128)(2,1)S(1)} %get-tuple-element.44.tiles, ...), custom_call_target="tpu_custom_call" | custom-call | flops 100000000 | bytes 4000000 | tf_op jit(solution)/shard_map/inner/pallas_call | solution.py:590
  43.9 1.9 %collective-permute-done.7.below = f32[16,2176]{1,0:T(8,128)S(1)} collective-permute-done((f32[16,2176]{1,0:T(8,128)S(1)}, f32[16,2176]{1,0:T(8,128)S(1)}, u32[]{:S(2)}, u32[]{:S(2)}) %collective-permute-start.7) | collective-permute-done | bytes 139296 | tf_op jit(solution)/shard_map/ppermute | solution.py:604
  45.9 0.3 collective-permute-done.6.above
  46.2 0.1 collective-permute-done.8
  46.3 3.4 %outer.3 = (f32[16,2176]{1,0:T(8,128)S(1)}, f32[16,16,128]{2,1,0:T(8,128)S(1)}, f32[16,16,128]{2,1,0:T(8,128)S(1)}, f32[16,16,128]{2,1,0:T(8,128)S(1)}, f32[16,128]{1,0:T(8,128)S(1)}) custom-call(s32[2]{0:T(128)S(1)} %pad_add_fusion.place, s32[8,256]{1,0:T(8,128)S(1)} %get-tuple-element.36.inner_plan.plan, s32[8,384]{1,0:T(8,128)S(1)} %get-tuple-element.42.plan, ...), custom_call_target="tpu_custom_call" | custom-call | flops 100000000 | bytes 4000000 | tf_op jit(solution)/shard_map/outer/pallas_call | solution.py:590
  49.7 2.1 %collective-permute-start.10 = (f32[16,2176]{1,0:T(8,128)S(1)}, f32[16,2176]{1,0:T(8,128)S(1)}, u32[]{:S(2)}, u32[]{:S(2)}) collective-permute-start(f32[16,2176]{1,0:T(8,128)S(1)} %get-tuple-element.53.after.mine), channel_id=1, source_target_pairs={{0,4},{4,8},{8,12},{12,0},{1,5},{5,9},{9,13},{13,1},{2,6},{6,10},{... | collective-permute-start | bytes 417800 | tf_op jit(solution)/shard_map/ppermute | solution.py:604
  51.9 1.7 %collective-permute-start.9 = (f32[16,2176]{1,0:T(8,128)S(1)}, f32[16,2176]{1,0:T(8,128)S(1)}, u32[]{:S(2)}, u32[]{:S(2)}) collective-permute-start(f32[16,2176]{1,0:T(8,128)S(1)} %get-tuple-element.53.after.mine), channel_id=1, source_target_pairs={{0,12},{4,0},{8,4},{12,8},{1,13},{5,1},{9,5},{13,9},{2,14},{6,2},{... | collective-permute-start | bytes 417800 | tf_op jit(solution)/shard_map/ppermute | solution.py:604
  53.6 0.2 points.1
  53.7 4.8 %slopes.1 = f32[256,128,128]{2,1,0:T(8,128)S(1)} custom-call(s32[8,256]{1,0:T(8,128)S(1)} %get-tuple-element.36.inner_plan.plan, s32[8,384]{1,0:T(8,128)S(1)} %get-tuple-element.42.plan, bf16[16,128,32]{2,1,0:T(8,128)(2,1)S(1)} %get-tuple-element.45.left.left_own, bf16[32,128,32]{2,1,0:T(8,128)(2,1)S(1)} %get-tuple-element.46.left.left_halo.left_out, ...), custom_call_target="tpu_custom_call" | custom-call | flops 300000000 | bytes 4000000 | tf_op jit(solution)/shard_map/slopes/pallas_call | solution.py:590
  58.6 7.7 %last.1.own = f32[19,2176]{1,0:T(8,128)S(1)} custom-call(s32[2]{0:T(128)S(1)} %pad_add_fusion.place, s32[8,256]{1,0:T(8,128)S(1)} %get-tuple-element.36.inner_plan.plan, s32[8,384]{1,0:T(8,128)S(1)} %get-tuple-element.42.plan, f32[16,2176]{1,0:T(8,128)S(1)} %get-tuple-element.53.after.mine, f32[16,2176]{1,0:T(8,128)S(1)} %collective-permute-done.9.above, ...), custom_call_target="tpu_custom_call" | custom-call | flops 300000000 | bytes 4000000 | tf_op jit(solution)/shard_map/last/pallas_call | solution.py:590
  66.4 1.4 %collective-permute-done.12.other = f32[19,2176]{1,0:T(8,128)S(1)} collective-permute-done((f32[19,2176]{1,0:T(8,128)S(1)}, f32[19,2176]{1,0:T(8,128)S(1)}, u32[]{:S(2)}, u32[]{:S(2)}) %collective-permute-start.12) | collective-permute-done | bytes 165408 | tf_op jit(solution)/shard_map/ppermute | solution.py:604
  67.9 1.5 %collective-permute-start.13 = (f32[3,2048]{1,0:T(4,128)S(1)}, f32[3,2048]{1,0:T(4,128)S(1)}, u32[]{:S(2)}, u32[]{:S(2)}) collective-permute-start(f32[3,2048]{1,0:T(4,128)S(1)} %pair.1), channel_id=1, source_target_pairs={{0,2},{2,0},{1,3},{3,1},{4,6},{6,4},{5,7},{7,5},{8,10},{10,8},{9,1... | collective-permute-start | bytes 73736 | tf_op jit(solution)/shard_map/ppermute | solution.py:604
  69.4 1.3 %close.1 = (f32[32,2048]{1,0:T(8,128)}, f32[3,32]{1,0:T(4,128)}, f32[3,32]{1,0:T(4,128)}) custom-call(s32[2]{0:T(128)S(1)} %pad_add_fusion.place, f32[19,2176]{1,0:T(8,128)S(1)} %last.1.own, f32[19,2176]{1,0:T(8,128)S(1)} %collective-permute-done.12.other), custom_call_target="tpu_custom_call" | custom-call | flops 1000000 | bytes 1000000 | tf_op jit(solution)/shard_map/close/pallas_call | solution.py:590
  70.7 1.2 %collective-permute-done.13 = f32[3,2048]{1,0:T(4,128)S(1)} collective-permute-done((f32[3,2048]{1,0:T(4,128)S(1)}, f32[3,2048]{1,0:T(4,128)S(1)}, u32[]{:S(2)}, u32[]{:S(2)}) %collective-permute-start.13) | collective-permute-done | bytes 24608 | tf_op jit(solution)/shard_map/ppermute | solution.py:604
  71.9 0.6 add.3
  (23 shorter events, 0.3 us)
Async XLA Ops:
  2.9 1.3 %collective-permute-start = (f32[8,128]{1,0:T(8,128)S(1)}, f32[8,128]{1,0:T(8,128)S(1)}, u32[]{:S(2)}, u32[]{:S(2)}) collective-permute-start(f32[8,128]{1,0:T(8,128)S(1)} %get-tuple-element.34), channel_id=1, source_target_pairs={{0,1},{1,0},{2,3},{3,2},{4,5},{5,4},{6,7},{7,6},{8,9},{9,8},{10,11... | collective-permute-start | bytes 12296 | tf_op jit(solution)/shard_map/ppermute | solution.py:604
  4.2 9.9 %collective-permute-start.2 = (f32[312,128]{1,0:T(8,128)S(1)}, f32[312,128]{1,0:T(8,128)S(1)}, u32[]{:S(2)}, u32[]{:S(2)}) collective-permute-start(f32[312,128]{1,0:T(8,128)S(1)} %join.1.mine.q_own.pts), channel_id=1, source_target_pairs={{0,4},{4,8},{8,12},{12,0},{1,5},{5,9},{9,13},{13,1},{2,6},{6,10},{... | collective-permute-start | bytes 479240 | tf_op jit(solution)/shard_map/ppermute | solution.py:604
  7.1 9.3 %collective-permute-start.1 = (f32[312,128]{1,0:T(8,128)S(1)}, f32[312,128]{1,0:T(8,128)S(1)}, u32[]{:S(2)}, u32[]{:S(2)}) collective-permute-start(f32[312,128]{1,0:T(8,128)S(1)} %join.1.mine.q_own.pts), channel_id=1, source_target_pairs={{0,12},{4,0},{8,4},{12,8},{1,13},{5,1},{9,5},{13,9},{2,14},{6,2},{... | collective-permute-start | bytes 479240 | tf_op jit(solution)/shard_map/ppermute | solution.py:604
  24.1 8.5 %collective-permute-start.4 = (f32[16,2176]{1,0:T(8,128)S(1)}, f32[16,2176]{1,0:T(8,128)S(1)}, u32[]{:S(2)}, u32[]{:S(2)}) collective-permute-start(f32[16,2176]{1,0:T(8,128)S(1)} %get-tuple-element.43.w_ref.mine), channel_id=1, source_target_pairs={{0,4},{4,8},{8,12},{12,0},{1,5},{5,9},{9,13},{13,1},{2,6},{6,10},{... | collective-permute-start | bytes 417800 | tf_op jit(solution)/shard_map/ppermute | solution.py:604
  25.5 8.5 %collective-permute-start.3 = (f32[16,2176]{1,0:T(8,128)S(1)}, f32[16,2176]{1,0:T(8,128)S(1)}, u32[]{:S(2)}, u32[]{:S(2)}) collective-permute-start(f32[16,2176]{1,0:T(8,128)S(1)} %get-tuple-element.43.w_ref.mine), channel_id=1, source_target_pairs={{0,12},{4,0},{8,4},{12,8},{1,13},{5,1},{9,5},{13,9},{2,14},{6,2},{... | collective-permute-start | bytes 417800 | tf_op jit(solution)/shard_map/ppermute | solution.py:604
  28.0 6.0 %collective-permute-start.5 = (f32[16,128]{1,0:T(8,128)S(1)}, f32[16,128]{1,0:T(8,128)S(1)}, u32[]{:S(2)}, u32[]{:S(2)}) collective-permute-start(f32[16,128]{1,0:T(8,128)S(1)} %get-tuple-element.69), channel_id=1, source_target_pairs={{0,8},{4,12},{8,0},{12,4},{1,9},{5,13},{9,1},{13,5},{2,10},{6,14},... | collective-permute-start | bytes 24584 | tf_op jit(solution)/shard_map/ppermute | solution.py:604
  37.5 8.4 %collective-permute-start.7 = (f32[16,2176]{1,0:T(8,128)S(1)}, f32[16,2176]{1,0:T(8,128)S(1)}, u32[]{:S(2)}, u32[]{:S(2)}) collective-permute-start(f32[16,2176]{1,0:T(8,128)S(1)} %get-tuple-element.47.w_ref.mine), channel_id=1, source_target_pairs={{0,4},{4,8},{8,12},{12,0},{1,5},{5,9},{9,13},{13,1},{2,6},{6,10},{... | collective-permute-start | bytes 417800 | tf_op jit(solution)/shard_map/ppermute | solution.py:604
  38.3 7.9 %collective-permute-start.6 = (f32[16,2176]{1,0:T(8,128)S(1)}, f32[16,2176]{1,0:T(8,128)S(1)}, u32[]{:S(2)}, u32[]{:S(2)}) collective-permute-start(f32[16,2176]{1,0:T(8,128)S(1)} %get-tuple-element.47.w_ref.mine), channel_id=1, source_target_pairs={{0,12},{4,0},{8,4},{12,8},{1,13},{5,1},{9,5},{13,9},{2,14},{6,2},{... | collective-permute-start | bytes 417800 | tf_op jit(solution)/shard_map/ppermute | solution.py:604
  41.3 5.0 %collective-permute-start.8 = (f32[16,128]{1,0:T(8,128)S(1)}, f32[16,128]{1,0:T(8,128)S(1)}, u32[]{:S(2)}, u32[]{:S(2)}) collective-permute-start(f32[16,128]{1,0:T(8,128)S(1)} %get-tuple-element.67), channel_id=1, source_target_pairs={{0,8},{4,12},{8,0},{12,4},{1,9},{5,13},{9,1},{13,5},{2,10},{6,14},... | collective-permute-start | bytes 24584 | tf_op jit(solution)/shard_map/ppermute | solution.py:604
  49.7 8.8 %collective-permute-start.10 = (f32[16,2176]{1,0:T(8,128)S(1)}, f32[16,2176]{1,0:T(8,128)S(1)}, u32[]{:S(2)}, u32[]{:S(2)}) collective-permute-start(f32[16,2176]{1,0:T(8,128)S(1)} %get-tuple-element.53.after.mine), channel_id=1, source_target_pairs={{0,4},{4,8},{8,12},{12,0},{1,5},{5,9},{9,13},{13,1},{2,6},{6,10},{... | collective-permute-start | bytes 417800 | tf_op jit(solution)/shard_map/ppermute | solution.py:604
  51.9 6.7 %collective-permute-start.9 = (f32[16,2176]{1,0:T(8,128)S(1)}, f32[16,2176]{1,0:T(8,128)S(1)}, u32[]{:S(2)}, u32[]{:S(2)}) collective-permute-start(f32[16,2176]{1,0:T(8,128)S(1)} %get-tuple-element.53.after.mine), channel_id=1, source_target_pairs={{0,12},{4,0},{8,4},{12,8},{1,13},{5,1},{9,5},{13,9},{2,14},{6,2},{... | collective-permute-start | bytes 417800 | tf_op jit(solution)/shard_map/ppermute | solution.py:604
  53.6 5.1 %collective-permute-start.11 = (f32[16,128]{1,0:T(8,128)S(1)}, f32[16,128]{1,0:T(8,128)S(1)}, u32[]{:S(2)}, u32[]{:S(2)}) collective-permute-start(f32[16,128]{1,0:T(8,128)S(1)} %get-tuple-element.65), channel_id=1, source_target_pairs={{0,8},{4,12},{8,0},{12,4},{1,9},{5,13},{9,1},{13,5},{2,10},{6,14},... | collective-permute-start | bytes 24584 | tf_op jit(solution)/shard_map/ppermute | solution.py:604
  66.3 1.5 %collective-permute-start.12 = (f32[19,2176]{1,0:T(8,128)S(1)}, f32[19,2176]{1,0:T(8,128)S(1)}, u32[]{:S(2)}, u32[]{:S(2)}) collective-permute-start(f32[19,2176]{1,0:T(8,128)S(1)} %last.1.own), channel_id=1, source_target_pairs={{0,1},{1,0},{2,3},{3,2},{4,5},{5,4},{6,7},{7,6},{8,9},{9,8},{10,11... | collective-permute-start | bytes 496136 | tf_op jit(solution)/shard_map/ppermute | solution.py:604
  67.9 4.0 %collective-permute-start.13 = (f32[3,2048]{1,0:T(4,128)S(1)}, f32[3,2048]{1,0:T(4,128)S(1)}, u32[]{:S(2)}, u32[]{:S(2)}) collective-permute-start(f32[3,2048]{1,0:T(4,128)S(1)} %pair.1), channel_id=1, source_target_pairs={{0,2},{2,0},{1,3},{3,1},{4,6},{6,4},{5,7},{7,5},{8,10},{10,8},{9,1... | collective-permute-start | bytes 73736 | tf_op jit(solution)/shard_map/ppermute | solution.py:604
where the time goes:
time: 72.8 us; the launch traced here: 72.5 us
  Pallas kernels  40 us (55%)
  starting transfers between devices  18.6 us (26%)
  waiting for transfers between devices  11.7 us (16%)
  between operations  1.4 us (2%)
    pallas_call x12, Pallas kernels, call(): pl.pallas_call(kernel, out_shape=tuple(out_shapes), in_specs=smem(scalars...  38.5 us
    ppermute x14, starting transfers between devices, shifted(): lax.ppermute(value, axes, [(source, (source + steps) % count) for source...  18.6 us
    ppermute x14, waiting for transfers between devices, shifted(): lax.ppermute(value, axes, [(source, (source + steps) % count) for source...  11.7 us
    pallas_call x1, Pallas kernels, body(): pl.pallas_call(functools.partial(pack_kernel, blocks), out_shape=(sds((LI...  1.52 us
  transfers between devices with their start and end apart: 14, of which 11 were waited for; matrix products, arithmetic and copies ran while one was open for 0% of the time, Pallas kernels for 22%

commit v1 on v0

--- a/solution.py
+++ b/solution.py
@@ -240,6 +240,13 @@
     ref[...] = jnp.zeros(ref.shape, ref.dtype)
     for at, row in enumerate(rows):
         ref[at : at + 1, :] = row.astype(ref.dtype)
+
+
+def to_smem(pairs, sems):
+    moves = [pltpu.make_async_copy(source, target, sems.at[at]) for at, (source, target) in enumerate(pairs)]
+    for move in moves:
+        move.start()
+    return moves
 
 
 def spread(row, width):
@@ -316,7 +323,7 @@
 
 def first_inner_kernel(
     blocks, mine,
-    plan, tiles, z_ref, cross, left, right, acc, vecs, held_plan, kinds, sem,
+    held_plan, tiles, z_ref, cross, left, right, acc, vecs, plan, kinds, sem,
 ):
     probes, coord_row, list_row = rows_of(mine, blocks)
     lists = mine[list_row:]
@@ -361,7 +368,7 @@
 
 def first_outer_kernel(
     blocks, inner_plan, old_tiles, mine, above, below, noise, z_ref, right, cross,
-    plan, tiles, w_ref, left, acc, vecs, held_plan, kinds, sem,
+    held_plan, tiles, w_ref, left, acc, vecs, inner_smem, plan, kinds, sems,
 ):
     probes, coord_row, list_row = rows_of(mine, blocks)
     del old_tiles
@@ -371,15 +378,15 @@
         held_plan,
         (cross[0:1] + row + blocks * one, cross[1:2] + col, cross[2:3] + times, spread(whole(end), slots)),
     )
-    move = pltpu.make_async_copy(held_plan, plan, sem)
-    move.start()
+    moves = to_smem(((inner_plan, inner_smem), (held_plan, plan)), sems)
     for part, ref in enumerate((above, below)):
         side_features(blocks, ref[coord_row:list_row], kinds, left.at[part * blocks : (part + 1) * blocks], None)
         for b in range(blocks):
             vecs[part * blocks + b] = stack_vec(ref[b * probes : (b + 1) * probes], True)
     acc[...] = jnp.zeros_like(acc)
-    move.wait()
-    base = inner_plan[3, 0]
+    for move in moves:
+        move.wait()
+    base = inner_smem[3, 0]
     fill(tiles, base, plan, maker(left, right))
     outer_edges(acc, vecs, plan, base, keeper(tiles), maker(left, right))
     finish_apply(
@@ -433,7 +440,7 @@
 
 
 def outer_kernel(
-    blocks, slabs, points, step, place, inner_plan, plan, mine, above, below, stats_ref,
+    blocks, slabs, points, step, place, held_inner, held_outer, mine, above, below, stats_ref,
     q_own, q_above, q_below, z_raw, z_old, noise, tiles, left, right, *rest,
 ):
     probes = mine.shape[0]
@@ -441,7 +448,8 @@
     if step > 0:
         old_ab = rest[0]
         rest = rest[1:]
-    w_ref, own_ref, above_ref, below_ref, ab_ref, *z_ref, acc, vecs, held_z = rest
+    w_ref, own_ref, above_ref, below_ref, ab_ref, *z_ref, acc, vecs, held_z, inner_plan, plan, sems = rest
+    moves = to_smem(((held_inner, inner_plan), (held_outer, plan)), sems)
     alpha, beta = global_alpha_beta(slabs, points, place, stats_ref)
     scale = 1.0 / beta
     apart = alpha - slab_alpha(mine, blocks)
@@ -459,6 +467,8 @@
                 for ref in z_ref:
                     ref[b] = z
     acc[...] = jnp.zeros_like(acc)
+    for move in moves:
+        move.wait()
     outer_edges(acc, vecs, plan, inner_plan[3, 0], keeper(tiles), maker(left, right))
     finish_apply(
         blocks, acc, lambda b: held_z[b], w_ref, lambda b: own_ref[b], lambda b: block_of(q_own, probes, b), beta, noise
@@ -497,15 +507,15 @@
 
 
 def last_kernel(
-    blocks, slabs, points, all_probes, place, inner_plan, plan, mine, above, below, stats_ref,
+    blocks, slabs, points, all_probes, place, held_inner, held_outer, mine, above, below, stats_ref,
     q_own, q_above, q_below, pts, pts_above, pts_below, old_ab, slopes, left_own, left_out, right, pnts, halo_pnts, slack,
-    out_ref, acc, form_left, halo_left, form_right, pulls,
+    basis_ref, grad_ref, acc, form_left, halo_left, form_right, pulls, inner_plan, plan, sems,
 ):
     probes, _, _ = rows_of(pts, blocks)
+    moves = to_smem(((held_inner, inner_plan), (held_outer, plan)), sems)
     alpha, beta = global_alpha_beta(slabs, points, place, stats_ref)
     scale = 1.0 / beta
-    out_ref[probes:, blocks * BLK :] = jnp.zeros((3, LANES), F32)
-    add_ab(out_ref.at[:probes], blocks * BLK, old_ab, ITERS - 1, alpha, beta)
+    add_ab(basis_ref, blocks * BLK, old_ab, ITERS - 1, alpha, beta)
     for part, (w, old, ref) in enumerate(((mine, q_own, pts), (above, q_above, pts_above), (below, q_below, pts_below))):
         for b in range(blocks):
             part_cols = slice(b * BLK, (b + 1) * BLK)
@@ -515,7 +525,7 @@
             low = u - high
             turned = jnp.concatenate([high, low, v, v], axis=0).T.astype(BF16)
             if part == 0:
-                out_ref[:probes, part_cols] = u
+                basis_ref[:, part_cols] = u
                 form_left[b] = turned
                 form_right[b] = jnp.concatenate([v, v, high, low], axis=0).astype(BF16)
             else:
@@ -527,6 +537,8 @@
     def pull_made(side, left):
         return lambda slot, a, c: stack_tile(mxu(side[a], form_right[c]) * slope_value(mxu(left[a], right[c])))
 
+    for move in moves:
+        move.wait()
     base = inner_plan[3, 0]
     fill(pulls, 0, inner_plan, pull(form_left))
     fill(pulls, base, plan, pull(halo_left))
@@ -538,21 +550,20 @@
         chain = slack[pl.ds(3 * blocks + b, 3, stride=blocks), :]
         sums = acc[b]
         moved = sums[0:3] + sums[3:6] + sums[6:9] - x * sums[9:10]
-        out_ref[probes:, part_cols] = moved * chain * (1.0 / (LENGTH_SQ * all_probes))
-
-
-def pair_kernel(own, other, grad_ref):
-    probes = own.shape[0] - 3
-    width = grad_ref.shape[1]
-    grad_ref[...] = own[probes:, :width] + other[probes:, :width]
+        grad_ref[:, part_cols] = moved * chain * (1.0 / (LENGTH_SQ * all_probes))
+
+
+def pair_kernel(one, two, after, out):
+    del after
+    out[...] = one[...] + two[...]
 
 
 def close_kernel(place, own, other, basis_ref, alpha_ref, beta_ref):
-    probes = own.shape[0] - 3
+    probes = own.shape[0]
     width = basis_ref.shape[1]
     lower = place[1] == 0
-    mine = own[:probes]
-    theirs = other[:probes]
+    mine = own[...]
+    theirs = other[...]
     first = jnp.where(lower, mine, theirs)
     second = jnp.where(lower, theirs, mine)
     basis_ref[:probes] = first[:, :width]
@@ -651,6 +662,8 @@
     outer_slots = (blocks * (blocks + 1) + TAIL + LANES - 1) // LANES * LANES
     plan_shape = sds((LIST_ROWS, inner_slots), ints)
     outer_plan_shape = sds((LIST_ROWS, outer_slots), ints)
+    inner_smem = pltpu.SMEM((LIST_ROWS, inner_slots), ints)
+    outer_smem = pltpu.SMEM((LIST_ROWS, outer_slots), ints)
     slots = KEPT
     ext = width + LANES
     blocks_f32 = sds((blocks, probes, BLK), F32)
@@ -660,10 +673,10 @@
     inner_plan, tiles, z, cross, left_own, right = call(
         "first_inner",
         functools.partial(first_inner_kernel, blocks),
-        ((plan_shape, tile_shape, blocks_f32, sds((LIST_ROWS, outer_slots), F32), left_shape, right_shape), 1),
+        ((plan_shape, tile_shape, blocks_f32, sds((LIST_ROWS, outer_slots), F32), left_shape, right_shape), 0),
         ((mine,), 0),
         [
-            acc_shape, ((blocks, probes, 2 * BLK), BF16), ((LIST_ROWS, inner_slots), ints), kinds,
+            acc_shape, ((blocks, probes, 2 * BLK), BF16), inner_smem, kinds,
             pltpu.SemaphoreType.DMA,
         ],
         (WORK_FIRST, WORK_BYTES),
@@ -671,11 +684,11 @@
     outer_plan, tiles, w, left_halo = call(
         "first_outer",
         functools.partial(first_outer_kernel, blocks),
-        ((outer_plan_shape, tile_shape, sds((probes, ext), F32), sds((2 * blocks, BLK, FEATS), BF16)), 1),
-        ((inner_plan, held(tiles), mine, above, below, noise, z, right, cross), 1),
+        ((outer_plan_shape, tile_shape, sds((probes, ext), F32), sds((2 * blocks, BLK, FEATS), BF16)), 0),
+        ((inner_plan, held(tiles), mine, above, below, noise, z, right, cross), 0),
         [
-            acc_shape, ((2 * blocks, probes, 2 * BLK), BF16), ((LIST_ROWS, outer_slots), ints), kinds,
-            pltpu.SemaphoreType.DMA,
+            acc_shape, ((2 * blocks, probes, 2 * BLK), BF16), inner_smem, outer_smem, kinds,
+            pltpu.SemaphoreType.DMA((2,)),
         ],
         (WORK_FIRST, WORK_BYTES),
         {1: 1},
@@ -717,8 +730,11 @@
                 ),
                 0,
             ),
-            ((place, inner_plan, outer_plan, w, up, down, stats, *q, z_raw, z_old, noise, held(tiles), left_halo, right, *ab), 3),
-            [acc_shape, ((2 * blocks, 2 * probes, 2 * BLK), BF16), ((blocks, probes, BLK), F32)],
+            ((place, inner_plan, outer_plan, w, up, down, stats, *q, z_raw, z_old, noise, held(tiles), left_halo, right, *ab), 1),
+            [
+                acc_shape, ((2 * blocks, 2 * probes, 2 * BLK), BF16), ((blocks, probes, BLK), F32), inner_smem, outer_smem,
+                pltpu.SemaphoreType.DMA((2,)),
+            ],
             (WORK_NEXT, WORK_BYTES),
         )
         q = (q0, q1, q2)
@@ -747,16 +763,16 @@
         [((blocks * 16, BLK), F32)],
         (WORK_NEXT, WORK_BYTES),
     )
-    (result,) = call(
+    basis, grad = call(
         "last",
         functools.partial(last_kernel, blocks, slabs, points, all_probes),
-        ((sds((probes + 3, ext), F32),), 0),
+        ((sds((probes, ext), F32), sds((3, width), F32)), 0),
         (
             (
                 place, inner_plan, outer_plan, w, up, down, stats, *q, mine, above, below, *ab, held(slopes), left_own, left_halo,
                 right, pnts, halo_pnts, slack,
             ),
-            3,
+            1,
         ),
         [
             ((blocks, 16, BLK), F32),
@@ -764,17 +780,21 @@
             ((2 * blocks, BLK, 4 * probes), BF16),
             ((blocks, 4 * probes, BLK), BF16),
             ((slots, 2 * BLK, BLK), BF16),
+            inner_smem,
+            outer_smem,
+            pltpu.SemaphoreType.DMA((2,)),
         ],
         (WORK_FIRST, WORK_BYTES),
         limit=LIMIT_MIB * 3 // 2,
     )
 
-    other = shifted(result, "sub", subs, 1)
-    (grad,) = call("pair", pair_kernel, ((sds((3, width), F32),), 0), ((result, other), 0), [], (1000, 1000))
+    other = shifted(basis, "sub", subs, 1)
     if outer == 2:
-        coord_grad = grad + shifted(grad, "probe", outer, 1)
+        across = shifted(grad, "probe", outer, 1)
+        (grad,) = call("pair", pair_kernel, ((sds((3, width), F32),), 0), ((grad, across, other), 0), [], (1000, 1000))
     else:
-        coord_grad = lax.psum(grad, "probe")
+        grad = lax.psum(grad, "probe")
+    coord_grad = grad + shifted(grad, "sub", subs, 1)
     last_basis, alphas, betas = call(
         "close",
         close_kernel,
@@ -784,7 +804,7 @@
             ),
             0,
         ),
-        ((place, result, other), 1),
+        ((place, basis, other), 1),
         [],
         (1000000, 1000000),
     )

time: 72.8 us -> 71.4 us (0.981)
  the two profiles are of different devices: /device:TPU:0 before, /device:TPU:7 now
where the time goes in v1:
time: 71.4 us; the launch traced here: 70.2 us
  Pallas kernels  39.2 us (55%)
  starting transfers between devices  20 us (28%)
  waiting for transfers between devices  8.76 us (12%)
  between operations  1.5 us (2%)
    pallas_call x12, Pallas kernels, call(): pl.pallas_call(kernel, out_shape=tuple(out_shapes), in_specs=smem(scalars...  37.6 us
    ppermute x15, starting transfers between devices, shifted(): lax.ppermute(value, axes, [(source, (source + steps) % count) for source...  20 us
    ppermute x15, waiting for transfers between devices, shifted(): lax.ppermute(value, axes, [(source, (source + steps) % count) for source...  8.76 us
    pallas_call x1, Pallas kernels, body(): pl.pallas_call(functools.partial(pack_kernel, blocks), out_shape=(sds((LI...  1.52 us
  transfers between devices with their start and end apart: 15, of which 5 were waited for; matrix products, arithmetic and copies ran while one was open for 0% of the time, Pallas kernels for 22%

profile of v1, /device:TPU:7, one launch (start us, length us, event | category | flops | bytes accessed | tf_op | source)
XLA Modules:
  0.0 70.2 jit_solution(14240806527489915182)
XLA Ops:
  1.3 0.1 pad_add_fusion.place
  1.4 1.5 %pack.1 = (f32[8,128]{1,0:T(8,128)S(1)}, f32[312,128]{1,0:T(8,128)S(1)}, f32[16,128]{1,0:T(8,128)S(1)}) custom-call(s32[2]{0:T(128)S(1)} %pad_add_fusion.place, s32[1,96]{1,0:T(1,128)} %bitcast.32, s32[1,96]{1,0:T(1,128)} %bitcast.33, s32[1]{0:T(128)} %bitcast.27.tile_count, s32[32,2048]{1,0:T(8,128)} %signs.1, f32[3,2048]{1,0:T(4,128)} %coords.1, ...), custom_call_target="tpu_custom_call" | custom-call | tf_op jit(solution)/shard_map/pack/pallas_call | solution.py:637
  2.9 0.7 %collective-permute-start = (f32[8,128]{1,0:T(8,128)S(1)}, f32[8,128]{1,0:T(8,128)S(1)}, u32[]{:S(2)}, u32[]{:S(2)}) collective-permute-start(f32[8,128]{1,0:T(8,128)S(1)} %get-tuple-element.36), channel_id=1, source_target_pairs={{0,1},{1,0},{2,3},{3,2},{4,5},{5,4},{6,7},{7,6},{8,9},{9,8},{10,11... | collective-permute-start | bytes 12296 | tf_op jit(solution)/shard_map/ppermute | solution.py:615
  3.6 0.8 %collective-permute-done.sibling = f32[8,128]{1,0:T(8,128)S(1)} collective-permute-done((f32[8,128]{1,0:T(8,128)S(1)}, f32[8,128]{1,0:T(8,128)S(1)}, u32[]{:S(2)}, u32[]{:S(2)}) %collective-permute-start) | collective-permute-done | bytes 4128 | tf_op jit(solution)/shard_map/ppermute | solution.py:615
  4.5 1.3 %collective-permute-start.2 = (f32[312,128]{1,0:T(8,128)S(1)}, f32[312,128]{1,0:T(8,128)S(1)}, u32[]{:S(2)}, u32[]{:S(2)}) collective-permute-start(f32[312,128]{1,0:T(8,128)S(1)} %join.1.mine.q_own.pts), channel_id=1, source_target_pairs={{0,4},{4,8},{8,12},{12,0},{1,5},{5,9},{9,13},{13,1},{2,6},{6,10},{... | collective-permute-start | bytes 479240 | tf_op jit(solution)/shard_map/ppermute | solution.py:615
  5.7 2.0 %collective-permute-start.1 = (f32[312,128]{1,0:T(8,128)S(1)}, f32[312,128]{1,0:T(8,128)S(1)}, u32[]{:S(2)}, u32[]{:S(2)}) collective-permute-start(f32[312,128]{1,0:T(8,128)S(1)} %join.1.mine.q_own.pts), channel_id=1, source_target_pairs={{0,12},{4,0},{8,4},{12,8},{1,13},{5,1},{9,5},{13,9},{2,14},{6,2},{... | collective-permute-start | bytes 479240 | tf_op jit(solution)/shard_map/ppermute | solution.py:615
  7.8 4.0 %first_inner.1 = (s32[8,256]{1,0:T(8,128)S(1)}, bf16[256,256,128]{2,1,0:T(8,128)(2,1)S(1)}, f32[16,16,128]{2,1,0:T(8,128)S(1)}, f32[8,384]{1,0:T(8,128)S(1)}, bf...) custom-call(f32[312,128]{1,0:T(8,128)S(1)} %join.1.mine.q_own.pts), custom_call_target="tpu_custom_call" | custom-call | flops 300000000 | bytes 4000000 | tf_op jit(solution)/shard_map/first_inner/pallas_call | solution.py:601
  11.8 0.0 collective-permute-done.2.below.q_below.pts_below
  11.8 2.8 %collective-permute-done.1.above.q_above.pts_above = f32[312,128]{1,0:T(8,128)S(1)} collective-permute-done((f32[312,128]{1,0:T(8,128)S(1)}, f32[312,128]{1,0:T(8,128)S(1)}, u32[]{:S(2)}, u32[]{:S(2)}) %collective-permute-start.1) | collective-permute-done | bytes 159776 | tf_op jit(solution)/shard_map/ppermute | solution.py:615
  14.6 6.4 %first_outer.1 = (s32[8,384]{1,0:T(8,128)S(1)}, bf16[256,256,128]{2,1,0:T(8,128)(2,1)S(1)}, f32[16,2176]{1,0:T(8,128)S(1)}, bf16[32,128,32]{2,1,0:T(8,128)(2,1)S(1)}) custom-call(s32[8,256]{1,0:T(8,128)S(1)} %get-tuple-element.38.inner_plan.plan.held_inner, bf16[256,256,128]{2,1,0:T(8,128)(2,1)S(1)} %get-tuple-element.39.old_tiles, ...), custom_call_target="tpu_custom_call", output_to_operand_aliasing={{1}: (1, {})} | custom-call | flops 300000000 | bytes 4000000 | tf_op jit(solution)/shard_map/first_outer/pallas_call | solution.py:601
  21.1 0.3 collective-permute-start.4
  21.3 3.0 %collective-permute-start.3 = (f32[16,2176]{1,0:T(8,128)S(1)}, f32[16,2176]{1,0:T(8,128)S(1)}, u32[]{:S(2)}, u32[]{:S(2)}) collective-permute-start(f32[16,2176]{1,0:T(8,128)S(1)} %get-tuple-element.45.w_ref.mine), channel_id=1, source_target_pairs={{0,12},{4,0},{8,4},{12,8},{1,13},{5,1},{9,5},{13,9},{2,14},{6,2},{... | collective-permute-start | bytes 417800 | tf_op jit(solution)/shard_map/ppermute | solution.py:615
  24.4 0.0 collective-permute-start.5
  24.4 2.6 %inner.2.z_raw = f32[16,16,128]{2,1,0:T(8,128)S(1)} custom-call(s32[8,256]{1,0:T(8,128)S(1)} %get-tuple-element.38.inner_plan.plan.held_inner, f32[16,2176]{1,0:T(8,128)S(1)} %get-tuple-element.45.w_ref.mine, f32[312,128]{1,0:T(8,128)S(1)} %join.1.mine.q_own.pts, bf16[256,256,128]{2,1,0:T(8,128)(2,1)S(1)} %get-tuple-element.46.tiles, ...), custom_call_target="tpu_custom_call" | custom-call | flops 100000000 | bytes 4000000 | tf_op jit(solution)/shard_map/inner/pallas_call | solution.py:601
  27.0 1.3 %collective-permute-done.5 = f32[16,128]{1,0:T(8,128)S(1)} collective-permute-done((f32[16,128]{1,0:T(8,128)S(1)}, f32[16,128]{1,0:T(8,128)S(1)}, u32[]{:S(2)}, u32[]{:S(2)}) %collective-permute-start.5) | collective-permute-done | bytes 8224 | tf_op jit(solution)/shard_map/ppermute | solution.py:615
  28.3 3.9 %outer.2 = (f32[16,2176]{1,0:T(8,128)S(1)}, f32[16,16,128]{2,1,0:T(8,128)S(1)}, f32[16,16,128]{2,1,0:T(8,128)S(1)}, f32[16,16,128]{2,1,0:T(8,128)S(1)}, f32[16,1...) custom-call(s32[2]{0:T(128)S(1)} %pad_add_fusion.place, s32[8,256]{1,0:T(8,128)S(1)} %get-tuple-element.38.inner_plan.plan.held_inner, ...), custom_call_target="tpu_custom_call" | custom-call | flops 100000000 | bytes 4000000 | tf_op jit(solution)/shard_map/outer/pallas_call | solution.py:601
  32.2 1.5 %collective-permute-start.7 = (f32[16,2176]{1,0:T(8,128)S(1)}, f32[16,2176]{1,0:T(8,128)S(1)}, u32[]{:S(2)}, u32[]{:S(2)}) collective-permute-start(f32[16,2176]{1,0:T(8,128)S(1)} %get-tuple-element.49.w_ref.mine), channel_id=1, source_target_pairs={{0,4},{4,8},{8,12},{12,0},{1,5},{5,9},{9,13},{13,1},{2,6},{6,10},{... | collective-permute-start | bytes 417800 | tf_op jit(solution)/shard_map/ppermute | solution.py:615
  33.7 1.8 %collective-permute-start.6 = (f32[16,2176]{1,0:T(8,128)S(1)}, f32[16,2176]{1,0:T(8,128)S(1)}, u32[]{:S(2)}, u32[]{:S(2)}) collective-permute-start(f32[16,2176]{1,0:T(8,128)S(1)} %get-tuple-element.49.w_ref.mine), channel_id=1, source_target_pairs={{0,12},{4,0},{8,4},{12,8},{1,13},{5,1},{9,5},{13,9},{2,14},{6,2},{... | collective-permute-start | bytes 417800 | tf_op jit(solution)/shard_map/ppermute | solution.py:615
  35.5 2.6 %inner.3.z_raw = f32[16,16,128]{2,1,0:T(8,128)S(1)} custom-call(s32[8,256]{1,0:T(8,128)S(1)} %get-tuple-element.38.inner_plan.plan.held_inner, f32[16,2176]{1,0:T(8,128)S(1)} %get-tuple-element.49.w_ref.mine, f32[16,16,128]{2,1,0:T(8,128)S(1)} %get-tuple-element.50.q_own, bf16[256,256,128]{2,1,0:T(8,128)(2,1)S(1)} %get-tuple-element.46.tiles, ...), custom_call_target="tpu_custom_call" | custom-call | flops 100000000 | bytes 4000000 | tf_op jit(solution)/shard_map/inner/pallas_call | solution.py:601
  38.1 1.3 %collective-permute-done.6.above = f32[16,2176]{1,0:T(8,128)S(1)} collective-permute-done((f32[16,2176]{1,0:T(8,128)S(1)}, f32[16,2176]{1,0:T(8,128)S(1)}, u32[]{:S(2)}, u32[]{:S(2)}) %collective-permute-start.6) | collective-permute-done | bytes 139296 | tf_op jit(solution)/shard_map/ppermute | solution.py:615
  39.5 3.9 %outer.3 = (f32[16,2176]{1,0:T(8,128)S(1)}, f32[16,16,128]{2,1,0:T(8,128)S(1)}, f32[16,16,128]{2,1,0:T(8,128)S(1)}, f32[16,16,128]{2,1,0:T(8,128)S(1)}, f32[16,128]{1,0:T(8,128)S(1)}) custom-call(s32[2]{0:T(128)S(1)} %pad_add_fusion.place, s32[8,256]{1,0:T(8,128)S(1)} %get-tuple-element.38.inner_plan.plan.held_inner, ...), custom_call_target="tpu_custom_call" | custom-call | flops 100000000 | bytes 4000000 | tf_op jit(solution)/shard_map/outer/pallas_call | solution.py:601
  43.4 0.1 collective-permute-start.10
  43.4 3.2 %collective-permute-start.9 = (f32[16,2176]{1,0:T(8,128)S(1)}, f32[16,2176]{1,0:T(8,128)S(1)}, u32[]{:S(2)}, u32[]{:S(2)}) collective-permute-start(f32[16,2176]{1,0:T(8,128)S(1)} %get-tuple-element.55.after.mine), channel_id=1, source_target_pairs={{0,12},{4,0},{8,4},{12,8},{1,13},{5,1},{9,5},{13,9},{2,14},{6,2},{... | collective-permute-start | bytes 417800 | tf_op jit(solution)/shard_map/ppermute | solution.py:615
  46.7 0.2 points.1
  46.8 4.8 %slopes.1 = f32[256,128,128]{2,1,0:T(8,128)S(1)} custom-call(s32[8,256]{1,0:T(8,128)S(1)} %get-tuple-element.38.inner_plan.plan.held_inner, s32[8,384]{1,0:T(8,128)S(1)} %get-tuple-element.44.held_outer.plan, bf16[16,128,32]{2,1,0:T(8,128)(2,1)S(1)} %get-tuple-element.47.left.left_own, bf16[32,128,32]{2,1,0:T(8,128)(2,1)S(1)} %get-tuple-element.48.left.left_halo.left_out, ...), custom_call_target="tpu_custom_call" | custom-call | flops 300000000 | bytes 4000000 | tf_op jit(solution)/shard_map/slopes/pallas_call | solution.py:601
  51.7 8.0 %last.1 = (f32[16,2176]{1,0:T(8,128)S(1)}, f32[3,2048]{1,0:T(4,128)S(1)}) custom-call(s32[2]{0:T(128)S(1)} %pad_add_fusion.place, s32[8,256]{1,0:T(8,128)S(1)} %get-tuple-element.38.inner_plan.plan.held_inner, s32[8,384]{1,0:T(8,128)S(1)} %get-tuple-element.44.held_outer.plan, f32[16,2176]{1,0:T(8,128)S(1)} %get-tuple-element.55.after.mine, ...), custom_call_target="tpu_custom_call" | custom-call | flops 300000000 | bytes 4000000 | tf_op jit(solution)/shard_map/last/pallas_call | solution.py:601
  59.7 4.5 %collective-permute-start.12 = (f32[16,2176]{1,0:T(8,128)S(1)}, f32[16,2176]{1,0:T(8,128)S(1)}, u32[]{:S(2)}, u32[]{:S(2)}) collective-permute-start(f32[16,2176]{1,0:T(8,128)S(1)} %get-tuple-element.63.own), channel_id=1, source_target_pairs={{0,1},{1,0},{2,3},{3,2},{4,5},{5,4},{6,7},{7,6},{8,9},{9,8},{10,11... | collective-permute-start | bytes 417800 | tf_op jit(solution)/shard_map/ppermute | solution.py:615
  64.2 0.3 collective-permute-start.13
  64.5 2.5 %collective-permute-done.13.two = f32[3,2048]{1,0:T(4,128)S(1)} collective-permute-done((f32[3,2048]{1,0:T(4,128)S(1)}, f32[3,2048]{1,0:T(4,128)S(1)}, u32[]{:S(2)}, u32[]{:S(2)}) %collective-permute-start.13) | collective-permute-done | bytes 24608 | tf_op jit(solution)/shard_map/ppermute | solution.py:615
  67.0 1.3 %collective-permute-start.14 = (f32[3,2048]{1,0:T(4,128)S(1)}, f32[3,2048]{1,0:T(4,128)S(1)}, u32[]{:S(2)}, u32[]{:S(2)}) collective-permute-start(f32[3,2048]{1,0:T(4,128)S(1)} %pair.1), channel_id=1, source_target_pairs={{0,1},{1,0},{2,3},{3,2},{4,5},{5,4},{6,7},{7,6},{8,9},{9,8},{10,11... | collective-permute-start | bytes 73736 | tf_op jit(solution)/shard_map/ppermute | solution.py:615
  68.3 1.3 %close.1 = (f32[32,2048]{1,0:T(8,128)}, f32[3,32]{1,0:T(4,128)}, f32[3,32]{1,0:T(4,128)}) custom-call(s32[2]{0:T(128)S(1)} %pad_add_fusion.place, f32[16,2176]{1,0:T(8,128)S(1)} %get-tuple-element.63.own, f32[16,2176]{1,0:T(8,128)S(1)} %collective-permute-done.12.other.after), custom_call_target="tpu_custom_call" | custom-call | flops 1000000 | bytes 1000000 | tf_op jit(solution)/shard_map/close/pallas_call | solution.py:601
  69.6 0.6 add.3
  (25 shorter events, 0.1 us)
Async XLA Ops:
  2.9 1.6 %collective-permute-start = (f32[8,128]{1,0:T(8,128)S(1)}, f32[8,128]{1,0:T(8,128)S(1)}, u32[]{:S(2)}, u32[]{:S(2)}) collective-permute-start(f32[8,128]{1,0:T(8,128)S(1)} %get-tuple-element.36), channel_id=1, source_target_pairs={{0,1},{1,0},{2,3},{3,2},{4,5},{5,4},{6,7},{7,6},{8,9},{9,8},{10,11... | collective-permute-start | bytes 12296 | tf_op jit(solution)/shard_map/ppermute | solution.py:615
  4.5 7.4 %collective-permute-start.2 = (f32[312,128]{1,0:T(8,128)S(1)}, f32[312,128]{1,0:T(8,128)S(1)}, u32[]{:S(2)}, u32[]{:S(2)}) collective-permute-start(f32[312,128]{1,0:T(8,128)S(1)} %join.1.mine.q_own.pts), channel_id=1, source_target_pairs={{0,4},{4,8},{8,12},{12,0},{1,5},{5,9},{9,13},{13,1},{2,6},{6,10},{... | collective-permute-start | bytes 479240 | tf_op jit(solution)/shard_map/ppermute | solution.py:615
  5.7 8.9 %collective-permute-start.1 = (f32[312,128]{1,0:T(8,128)S(1)}, f32[312,128]{1,0:T(8,128)S(1)}, u32[]{:S(2)}, u32[]{:S(2)}) collective-permute-start(f32[312,128]{1,0:T(8,128)S(1)} %join.1.mine.q_own.pts), channel_id=1, source_target_pairs={{0,12},{4,0},{8,4},{12,8},{1,13},{5,1},{9,5},{13,9},{2,14},{6,2},{... | collective-permute-start | bytes 479240 | tf_op jit(solution)/shard_map/ppermute | solution.py:615
  21.1 5.9 %collective-permute-start.4 = (f32[16,2176]{1,0:T(8,128)S(1)}, f32[16,2176]{1,0:T(8,128)S(1)}, u32[]{:S(2)}, u32[]{:S(2)}) collective-permute-start(f32[16,2176]{1,0:T(8,128)S(1)} %get-tuple-element.45.w_ref.mine), channel_id=1, source_target_pairs={{0,4},{4,8},{8,12},{12,0},{1,5},{5,9},{9,13},{13,1},{2,6},{6,10},{... | collective-permute-start | bytes 417800 | tf_op jit(solution)/shard_map/ppermute | solution.py:615
  21.3 5.7 %collective-permute-start.3 = (f32[16,2176]{1,0:T(8,128)S(1)}, f32[16,2176]{1,0:T(8,128)S(1)}, u32[]{:S(2)}, u32[]{:S(2)}) collective-permute-start(f32[16,2176]{1,0:T(8,128)S(1)} %get-tuple-element.45.w_ref.mine), channel_id=1, source_target_pairs={{0,12},{4,0},{8,4},{12,8},{1,13},{5,1},{9,5},{13,9},{2,14},{6,2},{... | collective-permute-start | bytes 417800 | tf_op jit(solution)/shard_map/ppermute | solution.py:615
  24.4 3.9 %collective-permute-start.5 = (f32[16,128]{1,0:T(8,128)S(1)}, f32[16,128]{1,0:T(8,128)S(1)}, u32[]{:S(2)}, u32[]{:S(2)}) collective-permute-start(f32[16,128]{1,0:T(8,128)S(1)} %get-tuple-element.73), channel_id=1, source_target_pairs={{0,8},{4,12},{8,0},{12,4},{1,9},{5,13},{9,1},{13,5},{2,10},{6,14},... | collective-permute-start | bytes 24584 | tf_op jit(solution)/shard_map/ppermute | solution.py:615
  32.2 5.9 %collective-permute-start.7 = (f32[16,2176]{1,0:T(8,128)S(1)}, f32[16,2176]{1,0:T(8,128)S(1)}, u32[]{:S(2)}, u32[]{:S(2)}) collective-permute-start(f32[16,2176]{1,0:T(8,128)S(1)} %get-tuple-element.49.w_ref.mine), channel_id=1, source_target_pairs={{0,4},{4,8},{8,12},{12,0},{1,5},{5,9},{9,13},{13,1},{2,6},{6,10},{... | collective-permute-start | bytes 417800 | tf_op jit(solution)/shard_map/ppermute | solution.py:615
  33.7 5.8 %collective-permute-start.6 = (f32[16,2176]{1,0:T(8,128)S(1)}, f32[16,2176]{1,0:T(8,128)S(1)}, u32[]{:S(2)}, u32[]{:S(2)}) collective-permute-start(f32[16,2176]{1,0:T(8,128)S(1)} %get-tuple-element.49.w_ref.mine), channel_id=1, source_target_pairs={{0,12},{4,0},{8,4},{12,8},{1,13},{5,1},{9,5},{13,9},{2,14},{6,2},{... | collective-permute-start | bytes 417800 | tf_op jit(solution)/shard_map/ppermute | solution.py:615
  35.5 4.0 %collective-permute-start.8 = (f32[16,128]{1,0:T(8,128)S(1)}, f32[16,128]{1,0:T(8,128)S(1)}, u32[]{:S(2)}, u32[]{:S(2)}) collective-permute-start(f32[16,128]{1,0:T(8,128)S(1)} %get-tuple-element.71), channel_id=1, source_target_pairs={{0,8},{4,12},{8,0},{12,4},{1,9},{5,13},{9,1},{13,5},{2,10},{6,14},... | collective-permute-start | bytes 24584 | tf_op jit(solution)/shard_map/ppermute | solution.py:615
  43.4 8.3 %collective-permute-start.10 = (f32[16,2176]{1,0:T(8,128)S(1)}, f32[16,2176]{1,0:T(8,128)S(1)}, u32[]{:S(2)}, u32[]{:S(2)}) collective-permute-start(f32[16,2176]{1,0:T(8,128)S(1)} %get-tuple-element.55.after.mine), channel_id=1, source_target_pairs={{0,4},{4,8},{8,12},{12,0},{1,5},{5,9},{9,13},{13,1},{2,6},{6,10},{... | collective-permute-start | bytes 417800 | tf_op jit(solution)/shard_map/ppermute | solution.py:615
  43.4 8.2 %collective-permute-start.9 = (f32[16,2176]{1,0:T(8,128)S(1)}, f32[16,2176]{1,0:T(8,128)S(1)}, u32[]{:S(2)}, u32[]{:S(2)}) collective-permute-start(f32[16,2176]{1,0:T(8,128)S(1)} %get-tuple-element.55.after.mine), channel_id=1, source_target_pairs={{0,12},{4,0},{8,4},{12,8},{1,13},{5,1},{9,5},{13,9},{2,14},{6,2},{... | collective-permute-start | bytes 417800 | tf_op jit(solution)/shard_map/ppermute | solution.py:615
  46.7 5.0 %collective-permute-start.11 = (f32[16,128]{1,0:T(8,128)S(1)}, f32[16,128]{1,0:T(8,128)S(1)}, u32[]{:S(2)}, u32[]{:S(2)}) collective-permute-start(f32[16,128]{1,0:T(8,128)S(1)} %get-tuple-element.69), channel_id=1, source_target_pairs={{0,8},{4,12},{8,0},{12,4},{1,9},{5,13},{9,1},{13,5},{2,10},{6,14},... | collective-permute-start | bytes 24584 | tf_op jit(solution)/shard_map/ppermute | solution.py:615
  59.7 7.3 %collective-permute-start.12 = (f32[16,2176]{1,0:T(8,128)S(1)}, f32[16,2176]{1,0:T(8,128)S(1)}, u32[]{:S(2)}, u32[]{:S(2)}) collective-permute-start(f32[16,2176]{1,0:T(8,128)S(1)} %get-tuple-element.63.own), channel_id=1, source_target_pairs={{0,1},{1,0},{2,3},{3,2},{4,5},{5,4},{6,7},{7,6},{8,9},{9,8},{10,11... | collective-permute-start | bytes 417800 | tf_op jit(solution)/shard_map/ppermute | solution.py:615
  64.2 2.8 %collective-permute-start.13 = (f32[3,2048]{1,0:T(4,128)S(1)}, f32[3,2048]{1,0:T(4,128)S(1)}, u32[]{:S(2)}, u32[]{:S(2)}) collective-permute-start(f32[3,2048]{1,0:T(4,128)S(1)} %get-tuple-element.67.one), channel_id=1, source_target_pairs={{0,2},{2,0},{1,3},{3,1},{4,6},{6,4},{5,7},{7,5},{8,10},{10,8},{9,1... | collective-permute-start | bytes 73736 | tf_op jit(solution)/shard_map/ppermute | solution.py:615
  67.0 2.6 %collective-permute-start.14 = (f32[3,2048]{1,0:T(4,128)S(1)}, f32[3,2048]{1,0:T(4,128)S(1)}, u32[]{:S(2)}, u32[]{:S(2)}) collective-permute-start(f32[3,2048]{1,0:T(4,128)S(1)} %pair.1), channel_id=1, source_target_pairs={{0,1},{1,0},{2,3},{3,2},{4,5},{5,4},{6,7},{7,6},{8,9},{9,8},{10,11... | collective-permute-start | bytes 73736 | tf_op jit(solution)/shard_map/ppermute | solution.py:615
